TPU v7x, 32 devices: a whole 2x2x4 slice. The times are simulated.
32 devices in a mesh: groups: 2 (over x), seq: 16 (over z, y, core).
Axes of the slice: x: 2, y: 2, z: 4, core: 2. Of those that a mesh axis runs over, the one named last changes fastest.
Arguments:
- features: bfloat16 [4096, 2048], P(('groups', 'seq')), parts along dimension 0, may hold values from -40 to 40
- state_write: bfloat16 [4096, 64], P(('groups', 'seq')), parts along dimension 0, may hold values from -0.75 to 0.75
- state_read: bfloat16 [4096, 64], P(('groups', 'seq')), parts along dimension 0, may hold values from -0.75 to 0.75
- log_decay: float32 [4096, 32], P(('groups', 'seq')), parts along dimension 0, may hold values from -2 to 0
- skip_gain: float32 [32], replicated, may hold values from 1 to 4
- post_gain: float32 [2048], replicated, may hold values from 0.5 to 2
- start_index: int32 [4096], P(('groups', 'seq')), parts along dimension 0, may hold values from 0 to 2047, as said below
- step_noise: bfloat16 [3, 4096, 1024], P(None, ('groups', 'seq')), parts along dimension 1, may hold values from -4 to 4
- act_weight: bfloat16 [2048, 128], replicated, may hold values from -0.125 to 0.125
- dyn_weight: bfloat16 [2048, 1024], replicated, may hold values from -0.125 to 0.125
- act_in_weight: bfloat16 [128, 1024], replicated, may hold values from -0.5 to 0.5
- out_weight: bfloat16 [1024, 2048], replicated, may hold values from -0.1875 to 0.1875
- value_weight: bfloat16 [1024], replicated, may hold values from -0.1875 to 0.1875
Outputs:
- posterior: bfloat16 [4096, 2048], P(('groups', 'seq')), parts along dimension 0
- values: float32 [3, 4096], P(None, ('groups', 'seq')), parts along dimension 1
- final_latent: bfloat16 [4096, 2048], P(('groups', 'seq')), parts along dimension 0
There are 2 independent parts, one for each index of `groups`. A program takes and returns all parts, laid end to end along the dimension named above; an argument that names none is the same for every part. Nothing has to cross between parts.
Inputs may be any that keep to these rules, and one draw needn't show every extreme that they name: `start_index`: each aligned block of 128 starts (the starts of one device) names exactly 8 time steps in every aligned range of 128 time steps.
All inputs are finite; a program needn't handle non-finite values.
Results may differ from a plain program's by a relative error of at most 0.01.
Values may be sent and summed in bfloat16 or wider, within the bound.
A program may use at most 192 MiB of HBM per device.

v0:
```python
import jax
import jax.numpy as jnp
from jax import lax
from jax.sharding import PartitionSpec as P


def entering(shard, axis, combine, identity):
    count, mine = (lax.axis_size(axis), lax.axis_index(axis))
    everything = jax.tree.map(lambda part: lax.all_gather(part, axis), shard)
    start = jax.tree.map(
        lambda part, zero: jnp.broadcast_to(jnp.asarray(zero, part.dtype), part.shape),
        shard,
        identity,
    )

    def lap(k, before):
        reached = k < mine
        new = combine(before, jax.tree.map(lambda part: part[k], everything))
        return jax.tree.map(lambda a, b: jnp.where(reached, a, b), new, before)

    return lax.fori_loop(0, count, lap, start)


def lower_ones(count):
    positions = jnp.arange(count, dtype=jnp.int32)
    return (positions[:, None] >= positions[None, :]).astype(jnp.float32)


def local_pass(wide_in, write_in, read_in, decay_in):
    row_count, width = wide_in.shape
    head_count = decay_in.shape[1]
    head_width = width // head_count
    block = min(256, row_count)
    block_count = row_count // block
    positions = jnp.arange(block, dtype=jnp.int32)
    lower_mask = positions[:, None] >= positions[None, :]
    lower_table = lower_mask.astype(jnp.float32)

    def advance(state_now, inputs):
        x_block, write_block, read_block, decay_block = inputs
        running = jnp.dot(lower_table, decay_block, precision=lax.Precision.HIGHEST)
        running_t = running.T
        spread = running_t[:, :, None] - running_t[:, None, :]
        weight = jnp.exp(jnp.where(lower_mask[None], spread, -jnp.inf))
        gram = jnp.dot(read_block, write_block.T, preferred_element_type=jnp.float32)
        inner_part = jnp.einsum(
            "hts,shp->thp",
            weight * gram[None],
            x_block.reshape(block, head_count, head_width),
            precision=lax.Precision.HIGHEST,
        ).reshape(block, width)
        read_wide = read_block.astype(jnp.float32)
        carried = jnp.dot(read_wide, state_now, precision=lax.Precision.HIGHEST) * jnp.repeat(
            jnp.exp(running), head_width, axis=1
        )
        tail = jnp.repeat(jnp.exp(running[-1:] - running), head_width, axis=1)
        whole_decay = jnp.repeat(jnp.exp(running[-1]), head_width)
        added = jnp.einsum(
            "sn,sd->nd",
            write_block.astype(jnp.float32),
            x_block * tail,
            precision=lax.Precision.HIGHEST,
        )
        state_next = state_now * whole_decay[None, :] + added
        return (state_next, inner_part + carried)

    zero_state = jnp.zeros((write_in.shape[1], width), jnp.float32)
    inputs = (
        wide_in.reshape(block_count, block, width),
        write_in.reshape(block_count, block, write_in.shape[1]),
        read_in.reshape(block_count, block, read_in.shape[1]),
        decay_in.reshape(block_count, block, head_count),
    )
    end_state, outputs = lax.scan(advance, zero_state, inputs)
    return (end_state, outputs.reshape(row_count, width))


def join_states(earlier, later):
    grow = jnp.repeat(later[0], earlier[1].shape[1] // later[0].shape[0])
    return (earlier[0] * later[0], earlier[1] * grow[None, :] + later[1])


def regroup_rows(posterior, start_index):
    row_count = posterior.shape[0]
    peer_count = lax.axis_size("seq")
    start_count = start_index.shape[0]
    slot_cap = start_count // peer_count
    owners = start_index // row_count
    offset = start_index % row_count
    owner_hits = (owners[:, None] == jnp.arange(peer_count, dtype=jnp.int32)[None, :]).astype(
        jnp.float32
    )
    running_hits = jnp.dot(lower_ones(start_count), owner_hits, precision=lax.Precision.HIGHEST)
    slot_rank = jnp.sum(running_hits * owner_hits, axis=1).astype(jnp.int32) - 1
    slot_index = owners * slot_cap + slot_rank
    wanted = (
        jnp.zeros((peer_count * slot_cap,), jnp.int32)
        .at[slot_index]
        .set(offset)
        .reshape(peer_count, slot_cap)
    )
    picked = jnp.take(
        posterior, lax.all_to_all(wanted, "seq", split_axis=0, concat_axis=0, tiled=True), axis=0
    )
    landed = lax.all_to_all(picked, "seq", split_axis=0, concat_axis=0, tiled=True)
    return jnp.take(landed.reshape(peer_count * slot_cap, posterior.shape[1]), slot_index, axis=0)


def imagine(latent, step_noise, act_weight, dyn_weight, act_in_weight, out_weight, value_weight):
    value_list = []
    for step_idx in range(step_noise.shape[0]):
        wide = latent.astype(jnp.float32)
        normed = (wide * lax.rsqrt(jnp.mean(wide * wide, axis=-1, keepdims=True) + 1e-06)).astype(
            jnp.bfloat16
        )
        action = jnp.tanh(jnp.dot(normed, act_weight, preferred_element_type=jnp.float32)).astype(
            jnp.bfloat16
        )
        inner = jnp.dot(normed, dyn_weight, preferred_element_type=jnp.float32) + jnp.dot(
            action, act_in_weight, preferred_element_type=jnp.float32
        )
        hidden = (jax.nn.silu(inner) + step_noise[step_idx].astype(jnp.float32)).astype(
            jnp.bfloat16
        )
        value_list.append(jnp.dot(hidden, value_weight, preferred_element_type=jnp.float32))
        latent = (wide + jnp.dot(hidden, out_weight, preferred_element_type=jnp.float32)).astype(
            jnp.bfloat16
        )
    return (jnp.stack(value_list), latent)


def per_device(
    features,
    state_write,
    state_read,
    log_decay,
    skip_gain,
    post_gain,
    start_index,
    step_noise,
    act_weight,
    dyn_weight,
    act_in_weight,
    out_weight,
    value_weight,
):
    row_count, width = features.shape
    head_count = log_decay.shape[1]
    head_width = width // head_count
    wide_in = features.astype(jnp.float32)
    end_state, local_out = local_pass(wide_in, state_write, state_read, log_decay)
    shard_decay = jnp.exp(jnp.sum(log_decay, axis=0))
    identity = (jnp.ones((head_count,), jnp.float32), jnp.zeros_like(end_state))
    _, carry_in = entering((shard_decay, end_state), "seq", join_states, identity)
    entered = jnp.exp(jnp.dot(lower_ones(row_count), log_decay, precision=lax.Precision.HIGHEST))
    from_before = jnp.dot(
        state_read.astype(jnp.float32), carry_in, precision=lax.Precision.HIGHEST
    ) * jnp.repeat(entered, head_width, axis=1)
    mixed = local_out + from_before + jnp.repeat(skip_gain, head_width)[None, :] * wide_in
    head_table = (
        jnp.arange(width, dtype=jnp.int32)[:, None] // head_width
        == jnp.arange(head_count, dtype=jnp.int32)[None, :]
    ).astype(jnp.float32)
    square_mean = jnp.dot(mixed * mixed, head_table, precision=lax.Precision.HIGHEST) / head_width
    scale = jnp.repeat(lax.rsqrt(square_mean + 1e-05), head_width, axis=1)
    posterior = (mixed * scale * post_gain[None, :]).astype(jnp.bfloat16)
    latent = regroup_rows(posterior, start_index)
    values, final_latent = imagine(
        latent, step_noise, act_weight, dyn_weight, act_in_weight, out_weight, value_weight
    )
    return (posterior, values, final_latent)


def solution(mesh):
    placed = (
        P(("groups", "seq"), None),
        P(("groups", "seq"), None),
        P(("groups", "seq"), None),
        P(("groups", "seq"), None),
        P(),
        P(),
        P(("groups", "seq")),
        P(None, ("groups", "seq"), None),
        P(),
        P(),
        P(),
        P(),
        P(),
    )
    return jax.shard_map(
        per_device,
        mesh=mesh,
        in_specs=placed,
        out_specs=(
            P(("groups", "seq"), None),
            P(None, ("groups", "seq")),
            P(("groups", "seq"), None),
        ),
        check_vma=False,
    )
```

profile of v0, /device:TPU:0, one launch (start us, length us, event | category | flops | bytes accessed | tf_op | source)
XLA Modules:
  0.0 166.1 jit_solution(9370423981715717801)
XLA Ops:
  7.3 0.9 fusion.44
  8.2 0.2 slice_reduce_fusion
  8.7 1.3 copy.32
  10.1 2.3 %fusion.11 = f32[64,2048]{1,0:T(8,128)} fusion(bf16[128,64]{0,1:T(8,128)(2,1)} %param.16, f32[128,2048]{0,1:T(8,128)S(1)} %bitcast.98, bf16[128,2048]{0,1:T(8,128)(2,1)S(1)} %copy.32, f32[2048]{0:T(1024)S(1)} %mul.144), kind=kOutput, calls=%fused_computation.22 | convolution fusion | flops 201981952 | bytes 2121728 | tf_op jit(solution)/shard_map/while/body/eval_jaxpr/sn,sd->nd/dot_general | solution.py:58
  12.6 1.0 scatter_custom_fusion
  13.6 0.7 all_to_all.13
  14.3 7.4 %all-to-all-start = ((s32[16,1,8]{2,1,0:T(1,128)}), s32[16,1,8]{2,1,0:T(1,128)S(1)}, u32[]{:S(2)}, u32[]{:S(2)}) async-start(s32[16,1,8]{2,1,0:T(1,128)} %bitcast.12), calls=%async_computation | async-start | bytes 16384 | tf_op jit(solution)/shard_map/all_to_all | solution.py:103
  21.8 0.6 dynamic-slice.5
  23.4 2.5 %fusion.12 = f32[32,128,64]{1,2,0:T(8,128)S(1)} fusion(bf16[128,32,64]{0,2,1:T(8,128)(2,1)S(1)} %bitcast.97, f32[128,128]{1,0:T(8,128)S(1)} %fusion.53, f32[32,128]{1,0:T(8,128)S(1)} %bitcast.101, pred[128,128]{1,0:T(8,128)(4,1)S(1)} %iota_compare_fusion.2), kind=kOutput, calls=%fused_computation.23 | convolution fusion | flops 404226048 | bytes 1671168 | tf_op jit(solution)/shard_map/while/body/eval_jaxpr/hts,shp->thp/dot_general | solution.py:46
  26.0 1.6 fusion.5
  27.6 34.6 %all-reduce = f32[512]{0:T(512)S(1)} all-reduce(f32[512]{0:T(512)S(1)} %exponential_dynamic-update-slice_fusion), channel_id=2, replica_groups=mesh['groups'=2,'seq'=16] {'seq'}, use_global_device_ids=true, to_apply=%add | all-reduce | flops 512 | bytes 4096
  62.8 27.5 %all-gather.4.cloned.1.call-done = f32[1024,2048]{1,0:T(8,128)} async-done(((f32[64,2048]{1,0:T(8,128)}), f32[1024,2048]{1,0:T(8,128)}) %all-gather.4.cloned.1.call-update) | async-done | bytes 8388624 | tf_op jit(solution)/shard_map/all_gather | solution.py:9
  90.3 26.5 %while.9 = (s32[]{:T(128)}, f32[64,2048]{1,0:T(8,128)S(1)}, s32[]{:T(128)}, f32[16,32]{1,0:T(8,128)S(1)}, f32[16,64,2048]{2,1,0:T(8,128)}, /*index=5*/s32[]{:T(128)}, s32[]{:T(128)}) while((s32[]{:T(128)}, f32[64,2048]{1,0:T(8,128)S(1)}, s32[]{:T(128)}, f32[16,32]{1,0:T(8,128)S(1)}, f32[16,64,2048]{2,1,0:T(8,128)}, ...), condition=%wide.region_2.3_spmd.clone, body=%wide.region_1.2_spmd.clone.sunk | while | flops 524292 | bytes 1606121 | solution.py:21
  90.5 1.5 fusion.87
  92.1 1.5 fusion.87
  93.8 1.5 fusion.87
  95.4 1.5 fusion.87
  97.1 1.5 fusion.87
  98.8 1.5 fusion.87
  100.4 1.5 fusion.87
  102.1 1.5 fusion.87
  103.7 1.5 fusion.87
  105.4 1.5 fusion.87
  107.1 1.5 fusion.87
  108.7 1.5 fusion.87
  110.4 1.5 fusion.87
  112.0 1.5 fusion.87
  113.7 1.5 fusion.87
  115.3 1.5 fusion.87
  116.8 2.5 %fusion.3 = f32[128,2048]{0,1:T(8,128)S(1)} fusion(f32[128,2048]{0,1:T(8,128)} %fusion.5, f32[128,2048]{0,1:T(8,128)S(1)} %bitcast.96, f32[64,2048]{1,0:T(8,128)S(1)} %get-tuple-element.124, bf16[128,64]{0,1:T(8,128)(2,1)S(1)} %copy-done.8, bf16[128,2048]{0,1:T(8,128)(2,1)S(1)} %copy.32, f32[2048]{0:T(1024)S(1)} %mul.148), kind=kOutput, calls=%fused_computation.12 | convolution fusion | flops 202637312 | bytes 4218880 | tf_op jit(solution)/shard_map/dot_general | solution.py:156
  119.3 1.3 fusion.24
  120.7 0.3 fusion.29
  121.3 0.9 gather_fusion
  122.2 0.9 bitcast_select_fusion
  123.1 3.8 %all-to-all-start.1 = ((bf16[16,8,2048]{2,1,0:T(8,128)(2,1)}), bf16[16,8,2048]{2,1,0:T(8,128)(2,1)S(1)}, u32[]{:S(2)}, u32[]{:S(2)}) async-start(bf16[16,8,2048]{2,1,0:T(8,128)(2,1)} %bitcast_select_fusion), calls=%async_computation.1 | async-start | bytes 1048576 | tf_op jit(solution)/shard_map/all_to_all | solution.py:105
  126.9 14.2 %all-to-all-done.1 = bf16[16,8,2048]{2,1,0:T(8,128)(2,1)S(1)} async-done(((bf16[16,8,2048]{2,1,0:T(8,128)(2,1)}), bf16[16,8,2048]{2,1,0:T(8,128)(2,1)S(1)}, u32[]{:S(2)}, u32[]{:S(2)}) %all-to-all-start.1) | async-done | bytes 524320 | tf_op jit(solution)/shard_map/all_to_all | solution.py:105
  141.1 0.9 gather_fusion.1
  142.1 0.3 fusion.26
  142.4 0.5 fusion.22
  143.0 3.3 %fusion.38 = bf16[128,1024]{1,0:T(8,128)(2,1)S(1)} fusion(f32[128,1024]{1,0:T(8,128)S(1)} %fusion.22, bf16[2048,1024]{1,0:T(8,128)(2,1)} %param.24, bf16[3,128,1024]{2,1,0:T(8,128)(2,1)} %param.22, f32[128]{0:T(128)S(1)} %add_rsqrt_fusion.2, bf16[128,2048]{1,0:T(8,128)(2,1)S(1)} %gather_fusion.1, pred[128]{0:T(512)(128)(4,1)S(1)} %get-tuple-element.162), kind=kOutput, calls=%fused_computation.70 | convolution fusion | flops 538968064 | bytes 5767808 | tf_op jit(solution)/shard_map/dot_general | solution.py:119
  146.5 1.0 multiply_reduce_fusion.1
  147.4 0.5 fusion.21
  148.0 3.3 %fusion.37 = bf16[128,1024]{1,0:T(8,128)(2,1)S(1)} fusion(f32[128,1024]{1,0:T(8,128)S(1)} %fusion.21, bf16[2048,1024]{1,0:T(8,128)(2,1)} %param.24, bf16[3,128,1024]{2,1,0:T(8,128)(2,1)} %param.22, f32[128,2048]{1,0:T(8,128)S(1)} %get-tuple-element.169, f32[128]{0:T(128)S(1)} %add_rsqrt_fusion.1), kind=kOutput, calls=%fused_computation.68 | convolution fusion | flops 538443776 | bytes 6291968 | tf_op jit(solution)/shard_map/dot_general | solution.py:119
  151.5 0.9 multiply_reduce_fusion
  152.4 0.5 fusion.20
  153.0 3.3 %fusion.36 = bf16[128,1024]{1,0:T(8,128)(2,1)S(1)} fusion(f32[128,1024]{1,0:T(8,128)S(1)} %fusion.20, bf16[2048,1024]{1,0:T(8,128)(2,1)} %param.24, bf16[3,128,1024]{2,1,0:T(8,128)(2,1)} %param.22, f32[128,2048]{1,0:T(8,128)S(1)} %get-tuple-element.171, f32[128]{0:T(128)S(1)} %add_rsqrt_fusion), kind=kOutput, calls=%fused_computation.66 | convolution fusion | flops 538443776 | bytes 6291968 | tf_op jit(solution)/shard_map/dot_general | solution.py:119
  156.5 1.6 fusion.10
  158.6 0.6 pad_maximum_fusion
  (118 shorter events, 5.5 us)
Async XLA Ops:
  7.2 135.2 %copy-start = (bf16[2048,128]{1,0:T(8,128)(2,1)S(1)}, bf16[2048,128]{1,0:T(8,128)(2,1)}, u32[]{:S(2)}) copy-start(bf16[2048,128]{1,0:T(8,128)(2,1)} %param.23) | copy-start | bytes 1572868
  7.2 14.6 %copy-start.15 = (u32[32]{0:T(128)S(1)}, u32[32]{0:T(128)}, u32[]{:S(2)}) copy-start(u32[32]{0:T(128)} %constant.141) | copy-start | bytes 388
  7.2 14.5 %copy-start.10 = (f32[128,32]{0,1:T(8,128)S(1)}, f32[128,32]{0,1:T(8,128)}, u32[]{:S(2)}) copy-start(f32[128,32]{0,1:T(8,128)} %param.18) | copy-start | bytes 49156
  7.2 16.0 %copy-start.9 = (bf16[128,64]{0,1:T(8,128)(2,1)S(1)}, bf16[128,64]{0,1:T(8,128)(2,1)}, u32[]{:S(2)}) copy-start(bf16[128,64]{0,1:T(8,128)(2,1)} %param.16) | copy-start | bytes 49156
  7.2 5.2 %copy-start.14 = (s32[128]{0:T(128)S(1)}, s32[128]{0:T(128)}, u32[]{:S(2)}) copy-start(s32[128]{0:T(128)} %param.21) | copy-start | bytes 1540
  7.2 16.0 %copy-start.8 = (bf16[128,64]{0,1:T(8,128)(2,1)S(1)}, bf16[128,64]{0,1:T(8,128)(2,1)}, u32[]{:S(2)}) copy-start(bf16[128,64]{0,1:T(8,128)(2,1)} %param.17) | copy-start | bytes 49156
  7.2 83.1 %all-gather.4.cloned.1.call-start = ((), (), s32[]{:S(2)}) async-start(), calls=%async_computation.2 | async-start | bytes 8912896 | tf_op jit(solution)/shard_map/all_gather | solution.py:9
  12.4 50.0 %copy-start.13 = (f32[32]{0:T(128)S(1)}, f32[32]{0:T(128)}, u32[]{:S(2)}) copy-start(f32[32]{0:T(128)} %param.19) | copy-start | bytes 388
  14.3 48.2 %all-to-all-start = ((s32[16,1,8]{2,1,0:T(1,128)}), s32[16,1,8]{2,1,0:T(1,128)S(1)}, u32[]{:S(2)}, u32[]{:S(2)}) async-start(s32[16,1,8]{2,1,0:T(1,128)} %bitcast.12), calls=%async_computation | async-start | bytes 16384 | tf_op jit(solution)/shard_map/all_to_all | solution.py:103
  116.8 3.8 %copy-start.11 = (f32[2048]{0:T(1024)S(1)}, f32[2048]{0:T(1024)}, u32[]{:S(2)}) copy-start(f32[2048]{0:T(1024)} %param.20) | copy-start | bytes 24580
  121.0 5.9 %copy-start.12 = (bf16[1024]{0:T(1024)(128)(2,1)S(1)}, bf16[1024]{0:T(1024)(128)(2,1)}, u32[]{:S(2)}) copy-start(bf16[1024]{0:T(1024)(128)(2,1)} %param.27) | copy-start | bytes 6148
  121.3 20.8 %copy-start.1 = (bf16[128,2048]{1,0:T(8,128)(2,1)}, bf16[128,2048]{1,0:T(8,128)(2,1)S(1)}, u32[]{:S(2)}) copy-start(bf16[128,2048]{1,0:T(8,128)(2,1)S(1)} %copy.40) | copy-start | bytes 1572868
  122.2 20.2 %copy-start.5 = (bf16[128,1024]{1,0:T(8,128)(2,1)S(1)}, bf16[128,1024]{1,0:T(8,128)(2,1)}, u32[]{:S(2)}) copy-start(bf16[128,1024]{1,0:T(8,128)(2,1)} %param.25) | copy-start | bytes 786436
  123.1 18.0 %all-to-all-start.1 = ((bf16[16,8,2048]{2,1,0:T(8,128)(2,1)}), bf16[16,8,2048]{2,1,0:T(8,128)(2,1)S(1)}, u32[]{:S(2)}, u32[]{:S(2)}) async-start(bf16[16,8,2048]{2,1,0:T(8,128)(2,1)} %bitcast_select_fusion), calls=%async_computation.1 | async-start | bytes 1048576 | tf_op jit(solution)/shard_map/all_to_all | solution.py:105
  142.9 3.5 %copy-start.2 = (bf16[1024,2048]{1,0:T(8,128)(2,1)S(1)}, bf16[1024,2048]{1,0:T(8,128)(2,1)}, u32[]{:S(2)}) copy-start(bf16[1024,2048]{1,0:T(8,128)(2,1)} %param.26) | copy-start | bytes 12582916
  148.0 3.5 %copy-start.3 = (bf16[1024,2048]{1,0:T(8,128)(2,1)S(1)}, bf16[1024,2048]{1,0:T(8,128)(2,1)}, u32[]{:S(2)}) copy-start(bf16[1024,2048]{1,0:T(8,128)(2,1)} %param.26) | copy-start | bytes 12582916
  151.5 0.9 copy-start.6
  153.0 3.5 %copy-start.4 = (bf16[1024,2048]{1,0:T(8,128)(2,1)S(1)}, bf16[1024,2048]{1,0:T(8,128)(2,1)}, u32[]{:S(2)}) copy-start(bf16[1024,2048]{1,0:T(8,128)(2,1)} %param.26) | copy-start | bytes 12582916
  156.5 1.7 %copy-start.7 = (bf16[128,1024]{1,0:T(8,128)(2,1)S(1)}, bf16[128,1024]{1,0:T(8,128)(2,1)}, u32[]{:S(2)}) copy-start(bf16[128,1024]{1,0:T(8,128)(2,1)} %copy-done.6) | copy-start | bytes 786436
Sparse Core Ops, SparseCore 0:
  12.5 77.7 all-gather.3
where the time goes:
time: 167 us; the launch traced here: 166 us
  waiting for transfers between devices  41.7 us (25%)
  blocking collectives  34.6 us (21%)
  matrix products  27 us (16%)
  other arithmetic  26.2 us (16%)
  between operations  15.1 us (9%)
  starting transfers between devices  11.2 us (7%)
  local copies, waits for them, and re-layouts  9.99 us (6%)
    unnamed x1, blocking collectives  34.6 us
    all_gather x1, waiting for transfers between devices, entering(): everything = jax.tree.map(lambda part: lax.all_gather(part, axis), shard)  27.5 us
    select_n x16, other arithmetic, lap(): return jax.tree.map(lambda a, b: jnp.where(reached, a, b), new, before)  23.7 us
    all_to_all x1, waiting for transfers between devices, regroup_rows(): lax.all_to_all(picked, 'seq', split_axis=0, concat_axis=0, tiled=True)  14.2 us
    dot_general x3, matrix products, imagine(): jnp.dot(normed, dyn_weight, preferred_element_type=jnp.float32)  9.93 us
    all_to_all x1, starting transfers between devices, regroup_rows(): lax.all_to_all(wanted, 'seq', split_axis=0, concat_axis=0, tiled=True)  7.38 us
    all_to_all x1, starting transfers between devices, regroup_rows(): lax.all_to_all(picked, 'seq', split_axis=0, concat_axis=0, tiled=True)  3.75 us
    dot_general x3, matrix products, imagine(): jnp.dot(hidden, out_weight, preferred_element_type=jnp.float32)  3.44 us
  transfers between devices with their start and end apart: 3, of which 2 were waited for; matrix products, arithmetic and copies ran while one was open for 4% of the time, Pallas kernels for 0%

commit v1 on v0

v1 whole, which is shorter than its diff:
```python
import functools
import jax
import jax.numpy as jnp
from jax import lax
from jax.experimental import pallas as pl
from jax.experimental.pallas import tpu as pltpu
from jax.sharding import PartitionSpec as P

F32 = jnp.float32
BF16 = jnp.bfloat16


def dot(a, b):
    return jnp.dot(a, b, preferred_element_type=F32)


def dot_nt(a, b):
    return lax.dot_general(a, b, (((1,), (1,)), ((), ())), preferred_element_type=F32)


def iota(shape, dim):
    return lax.broadcasted_iota(jnp.int32, shape, dim)


def plan(n, rows, width, state, starts):
    lanes = max(128, width // n)
    lane_blocks = width // lanes
    cuts = min(state // 16, n // lane_blocks)
    cap = starts // n
    pieces = max(1, 16 // cap)
    return lanes, lane_blocks, cuts, cap, pieces


def kernel(
    n,
    x_ref,
    write_ref,
    read_ref,
    decay_ref,
    skip_ref,
    gain_ref,
    start_ref,
    value_w_ref,
    noise_hbm,
    act_hbm,
    dyn_hbm,
    act_in_hbm,
    out_hbm,
    post_hbm,
    values_ref,
    final_hbm,
    noise,
    act_w,
    dyn_w,
    act_in_w,
    out_w,
    meta_out,
    meta_in,
    end_out,
    end_in,
    carry_out,
    carry_in,
    local,
    entered,
    post,
    pick_out,
    pick_in,
    latent,
    load_sem,
    post_sem,
    meta_s,
    meta_r,
    end_s,
    end_r,
    carry_s,
    carry_r,
    pick_s,
    pick_r,
):
    rows, width = x_ref.shape
    heads = decay_ref.shape[1]
    head_width = width // heads
    state = write_ref.shape[1]
    starts = start_ref.shape[1]
    lanes, lane_blocks, cuts, cap, pieces = plan(n, rows, width, state, starts)
    owners = lane_blocks * cuts
    depth = state // cuts
    slot_rows = pieces * cap
    piece_width = width // pieces
    me = lax.axis_index("seq")

    loads = [
        pltpu.make_async_copy(src, dst, load_sem.at[i])
        for i, (src, dst) in enumerate(
            (
                (act_hbm, act_w),
                (dyn_hbm, dyn_w),
                (act_in_hbm, act_in_w),
                (out_hbm, out_w),
                (noise_hbm, noise),
            )
        )
    ]
    for load in loads:
        load.start()

    barrier = pltpu.get_barrier_semaphore()

    def greet(j, _):
        pl.semaphore_signal(
            barrier,
            inc=1,
            device_id={"seq": lax.rem(me + j, n)},
            device_id_type=pl.DeviceIdType.MESH,
        )
        return 0

    lax.fori_loop(1, n, greet, 0)

    def remote(src, dst, send, recv, peer, slot):
        return pltpu.make_async_remote_copy(
            src_ref=src,
            dst_ref=dst,
            send_sem=send.at[peer],
            recv_sem=recv.at[slot],
            device_id={"seq": peer},
            device_id_type=pl.DeviceIdType.MESH,
        )

    lower = iota((rows, rows), 0) >= iota((rows, rows), 1)
    running = jnp.dot(
        lower.astype(F32),
        decay_ref[...],
        precision=lax.Precision.HIGHEST,
        preferred_element_type=F32,
    )
    spread = (iota((heads, width), 1) // head_width == iota((heads, width), 0)).astype(BF16)

    def widen(v):
        high = v.astype(BF16)
        low = (v - high.astype(F32)).astype(BF16)
        return dot(high, spread) + dot(low, spread)

    x_all = x_ref[...].astype(F32)
    tail = widen(jnp.exp(running[rows - 1 : rows] - running))
    eye_state = (iota((state, state), 0) == iota((state, state), 1)).astype(BF16)
    write_t = dot_nt(eye_state, write_ref[...]).astype(BF16)
    end_state = dot(write_t, (x_all * tail).astype(BF16))
    whole_decay = widen(jnp.exp(running[rows - 8 : rows]))[7:8]
    start_row = start_ref[...].astype(F32)
    for k in range(owners):
        at = slice((k // cuts) * lanes, (k // cuts + 1) * lanes)
        end_out[k] = end_state[(k % cuts) * depth : (k % cuts + 1) * depth, at].astype(BF16)
    meta_width = meta_out.shape[2]

    def padded(row):
        if row.shape[1] == meta_width:
            return row
        return jnp.concatenate([row, jnp.zeros((1, meta_width - row.shape[1]), F32)], axis=1)

    for k in range(n):
        block = min(k // cuts, lane_blocks - 1)
        meta_out[k, 0:1, :] = padded(start_row)
        meta_out[k, 1:2, :] = padded(whole_decay[:, block * lanes : (block + 1) * lanes])

    pl.semaphore_wait(barrier, n - 1)

    def send_first(j, _):
        peer = lax.rem(me + j, n)

        def send_end():
            remote(end_out.at[peer], end_in.at[me], end_s, end_r, peer, me).start()

        remote(meta_out.at[peer], meta_in.at[me], meta_s, meta_r, peer, me).start()
        if owners == n:
            send_end()
        else:
            pl.when(peer < owners)(send_end)
        return 0

    lax.fori_loop(1, n, send_first, 0)
    meta_in[pl.ds(me, 1)] = meta_out[pl.ds(me, 1)]

    def keep_own():
        end_in[pl.ds(me, 1)] = end_out[pl.ds(me, 1)]

    if owners == n:
        keep_own()
    else:
        pl.when(me < owners)(keep_own)

    running_t = running.T
    gram = dot_nt(read_ref[...], write_ref[...])
    skip = widen(jnp.broadcast_to(skip_ref[...], (8, heads)))[0:1]
    per_tile = 128 // head_width
    head_of = iota((rows, 128), 1) // head_width
    for tile in range(width // 128):
        at = slice(tile * 128, (tile + 1) * 128)
        x_tile = x_ref[:, at]
        total = x_tile.astype(F32) * skip[:, at]
        for inner in range(per_tile):
            h = tile * per_tile + inner
            gap = running[:, h : h + 1] - running_t[h : h + 1, :]
            weight = (jnp.exp(jnp.where(lower, gap, -jnp.inf)) * gram).astype(BF16)
            one_head = jnp.where(head_of == inner, x_tile.astype(F32), 0.0).astype(BF16)
            total = total + dot(weight, one_head)
        local[:, at] = total
    entered[...] = widen(jnp.exp(running))

    def fold():
        def lap(d, carry):
            carry_out[d] = carry.astype(BF16)

            @pl.when(d != me)
            def _():
                remote(carry_out.at[d], carry_in.at[me], carry_s, carry_r, d, me).start()
                remote(end_out.at[0], end_in.at[d], end_s, end_r, d, d).wait_recv()
                remote(meta_out.at[0], meta_in.at[d], meta_s, meta_r, d, d).wait_recv()

            return carry * meta_in[d, 1:2, :lanes] + end_in[d].astype(F32)

        lax.fori_loop(0, n, lap, jnp.zeros((depth, lanes), F32))
        carry_in[pl.ds(me, 1)] = carry_out[pl.ds(me, 1)]

    def only_meta():
        def lap(d, _):
            @pl.when(d != me)
            def _():
                remote(meta_out.at[0], meta_in.at[d], meta_s, meta_r, d, d).wait_recv()

            return 0

        lax.fori_loop(0, n, lap, 0)

    if owners == n:
        fold()
    else:
        pl.when(me < owners)(fold)
        pl.when(me >= owners)(only_meta)

    asked = meta_in[:, 0, :starts]
    base = (me * rows).astype(F32)
    hit = jnp.logical_and(asked >= base, asked < base + rows)
    up_to = (iota((starts, starts), 0) <= iota((starts, starts), 1)).astype(BF16)
    rank = dot(hit.astype(F32).astype(BF16), up_to)
    rank = jnp.where(hit, rank, 0.0).astype(BF16)
    offset = jnp.where(hit, asked - base, 0.0).astype(BF16)
    slots = n * slot_rows
    repeat = (iota((slots, n), 0) // slot_rows == iota((slots, n), 1)).astype(BF16)
    slot_at = iota((slots, starts), 0)
    chosen = dot(repeat, rank) == (slot_at % cap + 1).astype(F32)
    wanted = jnp.sum(jnp.where(chosen, dot(repeat, offset), 0.0), axis=1, keepdims=True)
    row_at = iota((slots, rows), 0)
    picks_row = wanted == iota((slots, rows), 1).astype(F32)
    picks = [
        jnp.where(jnp.logical_and(picks_row, (row_at // cap) % pieces == p), 1.0, 0.0).astype(BF16)
        for p in range(pieces)
    ]

    start_col = jnp.sum(
        jnp.where(iota((starts, starts), 0) == iota((starts, starts), 1), start_row, 0.0),
        axis=1,
        keepdims=True,
    )
    first = (iota((starts, n), 1) * rows).astype(F32)
    from_owner = jnp.logical_and(start_col >= first, start_col < first + rows)
    before = (iota((starts, starts), 0) >= iota((starts, starts), 1)).astype(BF16)
    count = dot(before, from_owner.astype(F32).astype(BF16))
    lands = jnp.sum(
        jnp.where(from_owner, count - 1.0 + (iota((starts, n), 1) * slot_rows).astype(F32), 0.0),
        axis=1,
        keepdims=True,
    )

    def carry_lap(k, _):
        @pl.when(k != me)
        def _():
            remote(carry_out.at[0], carry_in.at[k], carry_s, carry_r, k, k).wait_recv()

        return 0

    lax.fori_loop(0, owners, carry_lap, 0)
    same_head = jnp.where(
        iota((lanes, lanes), 0) // head_width == iota((lanes, lanes), 1) // head_width,
        1.0 / head_width,
        0.0,
    ).astype(BF16)
    read = read_ref[...]
    for block in range(lane_blocks):
        at = slice(block * lanes, (block + 1) * lanes)
        carry = carry_in[block * cuts : (block + 1) * cuts].reshape(state, lanes)
        mixed = local[:, at] + dot(read, carry) * entered[:, at]
        square_mean = dot((mixed * mixed).astype(BF16), same_head)
        post[:, at] = (mixed * lax.rsqrt(square_mean + 1e-05) * gain_ref[:, at]).astype(BF16)
    picked = dot(picks[0], post[:, :piece_width])
    for p in range(1, pieces):
        picked = picked + dot(picks[p], post[:, p * piece_width : (p + 1) * piece_width])
    pick_out[...] = picked.astype(BF16).reshape(n, slot_rows, piece_width)

    def send_rows(j, _):
        peer = lax.rem(me + j, n)
        remote(pick_out.at[peer], pick_in.at[me], pick_s, pick_r, peer, me).start()
        return 0

    lax.fori_loop(1, n, send_rows, 0)
    pick_in[pl.ds(me, 1)] = pick_out[pl.ds(me, 1)]
    post_copy = pltpu.make_async_copy(post, post_hbm, post_sem.at[0])
    post_copy.start()
    for load in loads:
        load.wait()

    def row_lap(j, _):
        peer = lax.rem(me + j, n)
        remote(pick_out.at[0], pick_in.at[peer], pick_s, pick_r, peer, peer).wait_recv()
        return 0

    lax.fori_loop(1, n, row_lap, 0)

    landed = pick_in[...].reshape(slots, piece_width)
    slot_of = iota((starts, slots), 1).astype(F32)
    for p in range(pieces):
        place = jnp.where(slot_of == lands + float(p * cap), 1.0, 0.0).astype(BF16)
        latent[:, p * piece_width : (p + 1) * piece_width] = dot(place, landed).astype(BF16)

    diagonal = iota((starts, starts), 0) == iota((starts, starts), 1)
    value_w = value_w_ref[...].astype(F32)
    for step in range(noise.shape[0]):
        wide = latent[...].astype(F32)
        normed = (
            wide * lax.rsqrt(jnp.mean(wide * wide, axis=-1, keepdims=True) + 1e-06)
        ).astype(BF16)
        action = jnp.tanh(dot(normed, act_w[...])).astype(BF16)
        inner = dot(normed, dyn_w[...]) + dot(action, act_in_w[...])
        hidden = (inner / (1.0 + jnp.exp(-inner)) + noise[step].astype(F32)).astype(BF16)
        value = jnp.sum(hidden.astype(F32) * value_w, axis=1, keepdims=True)
        values_ref[step : step + 1, :] = jnp.sum(
            jnp.where(diagonal, value, 0.0), axis=0, keepdims=True
        )
        latent[...] = (wide + dot(hidden, out_w[...])).astype(BF16)

    final_copy = pltpu.make_async_copy(latent, final_hbm, post_sem.at[1])
    final_copy.start()

    def sent(j, _):
        peer = lax.rem(me + j, n)
        remote(meta_out.at[0], meta_in.at[me], meta_s, meta_r, peer, me).wait_send()
        remote(pick_out.at[0], pick_in.at[me], pick_s, pick_r, peer, me).wait_send()

        def end_sent():
            remote(end_out.at[0], end_in.at[me], end_s, end_r, peer, me).wait_send()

        def carry_sent():
            remote(carry_out.at[0], carry_in.at[me], carry_s, carry_r, peer, me).wait_send()

        if owners == n:
            end_sent()
            carry_sent()
        else:
            pl.when(peer < owners)(end_sent)
            pl.when(me < owners)(carry_sent)
        return 0

    lax.fori_loop(1, n, sent, 0)
    post_copy.wait()
    final_copy.wait()


def per_device(
    features,
    state_write,
    state_read,
    log_decay,
    skip_gain,
    post_gain,
    start_index,
    step_noise,
    act_weight,
    dyn_weight,
    act_in_weight,
    out_weight,
    value_weight,
):
    n = lax.axis_size("seq")
    rows, width = features.shape
    state = state_write.shape[1]
    starts = start_index.shape[0]
    lanes, lane_blocks, cuts, cap, pieces = plan(n, rows, width, state, starts)
    owners, depth, slot_rows = lane_blocks * cuts, state // cuts, pieces * cap
    vmem = pl.BlockSpec(memory_space=pltpu.VMEM)
    hbm = pl.BlockSpec(memory_space=pl.ANY)
    sems = pltpu.SemaphoreType.DMA((n,))
    flops = 2 * step_noise.shape[0] * starts * (dyn_weight.size + out_weight.size)
    return pl.pallas_call(
        functools.partial(kernel, n),
        out_shape=(
            jax.ShapeDtypeStruct((rows, width), BF16),
            jax.ShapeDtypeStruct((step_noise.shape[0], starts), F32),
            jax.ShapeDtypeStruct((starts, width), BF16),
        ),
        in_specs=[vmem] * 8 + [hbm] * 5,
        out_specs=(hbm, vmem, hbm),
        scratch_shapes=[
            pltpu.VMEM(step_noise.shape, BF16),
            pltpu.VMEM(act_weight.shape, BF16),
            pltpu.VMEM(dyn_weight.shape, BF16),
            pltpu.VMEM(act_in_weight.shape, BF16),
            pltpu.VMEM(out_weight.shape, BF16),
            pltpu.VMEM((n, 8, max(lanes, starts)), F32),
            pltpu.VMEM((n, 8, max(lanes, starts)), F32),
            pltpu.VMEM((owners, depth, lanes), BF16),
            pltpu.VMEM((n, depth, lanes), BF16),
            pltpu.VMEM((n, depth, lanes), BF16),
            pltpu.VMEM((owners, depth, lanes), BF16),
            pltpu.VMEM((rows, width), F32),
            pltpu.VMEM((rows, width), F32),
            pltpu.VMEM((rows, width), BF16),
            pltpu.VMEM((n, slot_rows, width // pieces), BF16),
            pltpu.VMEM((n, slot_rows, width // pieces), BF16),
            pltpu.VMEM((starts, width), BF16),
            pltpu.SemaphoreType.DMA((5,)),
            pltpu.SemaphoreType.DMA((2,)),
            sems,
            sems,
            sems,
            sems,
            sems,
            sems,
            sems,
            sems,
        ],
        compiler_params=pltpu.CompilerParams(
            collective_id=0, has_side_effects=True, vmem_limit_bytes=56 * 1024 * 1024
        ),
        cost_estimate=pl.CostEstimate(
            flops=flops, bytes_accessed=12 * 1024 * 1024, transcendentals=1024 * 1024
        ),
    )(
        features,
        state_write,
        state_read,
        log_decay,
        skip_gain[None, :],
        post_gain[None, :],
        start_index[None, :],
        value_weight[None, :],
        step_noise,
        act_weight,
        dyn_weight,
        act_in_weight,
        out_weight,
    )


def solution(mesh):
    split = P(("groups", "seq"), None)
    placed = (
        split,
        split,
        split,
        split,
        P(),
        P(),
        P(("groups", "seq")),
        P(None, ("groups", "seq"), None),
        P(),
        P(),
        P(),
        P(),
        P(),
    )
    return jax.shard_map(
        per_device,
        mesh=mesh,
        in_specs=placed,
        out_specs=(split, P(None, ("groups", "seq")), split),
        check_vma=False,
    )
```

time: 167 us -> 53.9 us (0.32)
  the two profiles are of different devices: /device:TPU:0 before, /device:TPU:13 now
where the time goes in v1:
time: 53.9 us; the launch traced here: 53.4 us
  Pallas kernels  42.2 us (78%)
  local copies, waits for them, and re-layouts  10.6 us (20%)
  between operations  0.64 us (1%)
    pallas_call x1, Pallas kernels, per_device(): pl.pallas_call(functools.partial(kernel, n), out_shape=(jax.ShapeDtypeStr...  42.2 us
    unnamed x6, local copies, waits for them, and re-layouts  9.32 us
    broadcast_in_dim x1, local copies, waits for them, and re-layouts, per_device(): value_weight[None, :]  1.28 us

profile of v1, /device:TPU:13, one launch (start us, length us, event | category | flops | bytes accessed | tf_op | source)
XLA Modules:
  0.0 53.4 jit_solution(4808173629949703417)
XLA Ops:
  0.6 1.3 %broadcast_in_dim.15.value_w_ref = bf16[1,1024]{1,0:T(2,128)(2,1)} reshape(bf16[1024]{0:T(1024)(128)(2,1)} %param.25) | data formatting | bytes 4096 | tf_op jit(solution)/shard_map/broadcast_in_dim | solution.py:445
  1.9 1.4 %copy.16.write_ref = bf16[128,64]{1,0:T(8,128)(2,1)} copy(bf16[128,64]{0,1:T(8,128)(2,1)} %param.14) | data formatting | bytes 32768 | tf_op args[1]
  3.3 1.4 %copy.17.read_ref = bf16[128,64]{1,0:T(8,128)(2,1)} copy(bf16[128,64]{0,1:T(8,128)(2,1)} %param.15) | data formatting | bytes 32768 | tf_op args[2]
  4.8 1.4 %copy.18.decay_ref = f32[128,32]{1,0:T(8,128)} copy(f32[128,32]{0,1:T(8,128)} %param.16) | data formatting | bytes 32768 | tf_op args[3]
  6.2 42.2 %shard_map.148 = (bf16[128,2048]{1,0:T(8,128)(2,1)}, f32[3,128]{1,0:T(4,128)}, bf16[128,2048]{1,0:T(8,128)(2,1)}) custom-call(bf16[128,2048]{1,0:T(8,128)(2,1)} %x_ref.1, bf16[128,64]{1,0:T(8,128)(2,1)} %copy.16.write_ref, bf16[128,64]{1,0:T(8,128)(2,1)} %copy.17.read_ref, f32[128,32]{1,0:T(8,128)} %copy.18.decay_ref, f32[1,32]{1,0:T(1,128)} %bitcast.4, ...), custom_call_target="tpu_custom_call" | custom-call | flops 3221225472 | bytes 12582912 | tf_op jit(solution)/shard_map/pallas_call | solution.py:393
  48.4 1.9 %copy.22 = bf16[128,2048]{1,0:T(8,128)(2,1)} copy(bf16[128,2048]{1,0:T(8,128)(2,1)} %get-tuple-element.6) | data formatting | bytes 1048576
  50.3 1.3 %copy.23 = f32[3,128]{1,0:T(4,128)} copy(f32[3,128]{1,0:T(4,128)} %get-tuple-element.7) | data formatting | bytes 3072
  51.5 1.9 %copy.24 = bf16[128,2048]{1,0:T(8,128)(2,1)} copy(bf16[128,2048]{1,0:T(8,128)(2,1)} %get-tuple-element.8) | data formatting | bytes 1048576
